TPU v7x, 128 devices: a whole 4x4x4 slice. The times are simulated.
128 devices in a mesh: dp: 64 (over y, z_hi, x, core), pair: 2 (over z_lo).
Axes of the slice: x: 4, y: 4, z: 4 (z_hi: 2, z_lo: 2; z = z_hi * 2 + z_lo), core: 2. Of those that a mesh axis runs over, the one named last changes fastest.
Arguments:
- events: bfloat16 [65536, 2048], P(('dp', 'pair')), may hold values from -6 to 6
- w_uvqk: bfloat16 [2048, 4096], P(None, 'dp'), may hold values from -0.125 to 0.125
- w_out: bfloat16 [1024, 2048], P('dp'), may hold values from -0.1875 to 0.1875
- targets: bfloat16 [65536, 2048], P(('dp', 'pair')), may hold values from -0.125 to 0.125
- item_ids: int32 [65536], P(('dp', 'pair')), may hold values from 0 to 4095
- uniform_flags: int32 [65536], P(('dp', 'pair')), may hold values from 0 to 1, as said below
- lengths: int32 [128, 8], P(('dp', 'pair')), may hold values from 1 to 128, 512 in all within a row
- seq_weights: float32 [1024], P(('dp', 'pair')), may hold values from 0.2 to 5
Outputs:
- hyper: float32 [1024], P(('dp', 'pair'))
- weighted_grad: float32 [1024, 2048], P(('dp', 'pair'))
Inputs may be any that keep to these rules, and one draw needn't show every extreme that they name: `uniform_flags`: in every block of 512 events the first is flagged 1 and the last 0. Each row holds the lengths of one block's 8 sequences and sums to 512.
All inputs are finite; a program needn't handle non-finite values.
Results may differ from a plain program's by a relative error of at most 0.015.
Values may be sent and summed in bfloat16 or wider, within the bound.
No kernel may reach another device: no remote copies, remote signals or barrier semaphores. Data moves between devices by JAX's collectives and lax.ppermute only.
A program may use at most 128 MiB of HBM per device.

v0:
```python
import jax
import jax.numpy as jnp
from jax import lax
from jax.sharding import PartitionSpec as P

HEADS = 8
DH = 128


def on_device(events, w_uvqk, w_out, targets, item_ids, uniform_flags, lengths, seq_weights):
    count = events.shape[0]
    width = HEADS * DH
    seq_max = count // 4
    flag = uniform_flags.astype(jnp.float32)
    n_unif = lax.psum(jnp.sum(flag), ("dp", "pair"))
    n_train = jnp.float32(count * lax.axis_size("dp") * lax.axis_size("pair")) - n_unif
    pre = jnp.dot(
        events, lax.all_gather(w_uvqk, "dp", axis=1, tiled=True), preferred_element_type=jnp.float32
    )
    uvqk = jax.nn.silu(pre).astype(jnp.bfloat16)
    gate_u = uvqk[:, 0:width]
    vals = uvqk[:, width : 2 * width].reshape(count, HEADS, DH)
    query = uvqk[:, 2 * width : 3 * width].reshape(count, HEADS, DH)
    keys = uvqk[:, 3 * width : 4 * width].reshape(count, HEADS, DH)
    place = jnp.arange(count, dtype=jnp.int32)
    ends = jnp.cumsum(lengths[0])
    seqid = jnp.sum((place[:, None] >= ends[None, :]).astype(jnp.int32), axis=1)
    allowed = (seqid[:, None] == seqid[None, :]) & (place[:, None] >= place[None, :])
    scores_att = jnp.einsum(
        "ihd,jhd->hij", query, keys, preferred_element_type=jnp.float32
    ) / jnp.sqrt(jnp.float32(DH))
    probs = jnp.where(allowed[None], jax.nn.silu(scores_att) / seq_max, 0.0).astype(jnp.bfloat16)
    attn = jnp.einsum("hij,jhd->ihd", probs, vals, preferred_element_type=jnp.float32).reshape(
        count, width
    )
    mean = jnp.mean(attn, axis=1, keepdims=True)
    var = jnp.mean((attn - mean) ** 2, axis=1, keepdims=True)
    mixed = ((attn - mean) * lax.rsqrt(var + 1e-05) * gate_u.astype(jnp.float32)).astype(
        jnp.bfloat16
    )
    columns = mixed
    summed = jnp.dot(
        columns, lax.all_gather(w_out, "dp", axis=0, tiled=True), preferred_element_type=jnp.float32
    )
    outputs = (events.astype(jnp.float32) + summed).astype(jnp.bfloat16)
    scores = jnp.dot(outputs, targets.T, preferred_element_type=jnp.float32)
    diag = place[:, None] == place[None, :]
    other = item_ids[:, None] != item_ids[None, :]
    coef = jnp.where(
        diag, -jax.nn.sigmoid(-scores), jnp.where(other, jax.nn.sigmoid(scores) / count, 0.0)
    ).astype(jnp.bfloat16)
    grad_out = jnp.dot(coef, targets, preferred_element_type=jnp.float32).astype(jnp.bfloat16)
    member = (seqid[:, None] == jnp.arange(seq_weights.shape[0], dtype=jnp.int32)[None, :]).astype(
        jnp.float32
    )
    weight_row = jnp.sum(member * seq_weights[None, :], axis=1) * (1.0 - flag)
    scaled = (grad_out.astype(jnp.float32) * weight_row[:, None]).astype(jnp.bfloat16)
    unif_rows = grad_out * uniform_flags[:, None].astype(jnp.bfloat16)
    local_unif = lax.dot_general(
        mixed, unif_rows, (((0,), (0,)), ((), ())), preferred_element_type=jnp.float32
    )
    unif_sum = lax.psum(local_unif, ("dp", "pair"))
    unif_grad = unif_sum / n_unif
    unif_hi = unif_grad.astype(jnp.bfloat16)
    unif_lo = (unif_grad - unif_hi.astype(jnp.float32)).astype(jnp.bfloat16)
    proj = jnp.dot(grad_out, unif_hi.T, preferred_element_type=jnp.float32) + jnp.dot(
        grad_out, unif_lo.T, preferred_element_type=jnp.float32
    )
    per_row = -jnp.sum(mixed.astype(jnp.float32) * proj, axis=1) * (1.0 - flag)
    hyper = jnp.sum(member * per_row[:, None], axis=0)
    columns = mixed
    weighted_grad = (
        lax.psum_scatter(
            lax.dot_general(
                columns, scaled, (((0,), (0,)), ((), ())), preferred_element_type=jnp.float32
            ),
            ("dp", "pair"),
            scatter_dimension=0,
            tiled=True,
        )
        / n_train
    )
    return (hyper, weighted_grad)


def solution(mesh):
    return jax.shard_map(
        on_device,
        mesh=mesh,
        in_specs=(
            P(("dp", "pair"), None),
            P(None, "dp"),
            P("dp", None),
            P(("dp", "pair"), None),
            P(("dp", "pair")),
            P(("dp", "pair")),
            P(("dp", "pair"), None),
            P(("dp", "pair")),
        ),
        out_specs=(P(("dp", "pair")), P(("dp", "pair"), None)),
        check_vma=False,
    )
```

profile of v0, /device:TPU:0, one launch (start us, length us, event | category | flops | bytes accessed | tf_op | source)
XLA Modules:
  0.0 1042.9 jit_solution(7917456037995461957)
XLA Ops:
  7.2 0.0 copy-start
  7.2 0.0 all-gather.3.cloned.1.call-start
  7.2 0.7 all-gather.3.cloned.1.call-update
  7.9 0.0 all-gather.5.cloned.1.call-start
  8.0 0.7 all-gather.5.cloned.1.call-update
  8.7 0.0 all-reduce.2.cloned.1.call-start
  8.7 0.7 convert_element_type.63
  9.4 0.8 reduce-window.8
  10.2 0.1 convert_reduce_fusion
  10.3 0.2 fusion.23
  10.5 109.5 %all-gather.3.cloned.1.call-done = bf16[2048,4096]{0,1:T(8,128)(2,1)} async-done(((bf16[2048,64]{0,1:T(8,128)(2,1)}), bf16[2048,4096]{0,1:T(8,128)(2,1)}) %all-gather.3.cloned.1.call-update) | async-done | bytes 16777232 | tf_op jit(solution)/shard_map/all_gather | solution.py:18
  120.1 13.9 %multiply_convert_fusion = bf16[512,4096]{1,0:T(8,128)(2,1)S(1)} fusion(bf16[512,2048]{1,0:T(8,128)(2,1)} %param.8, bf16[2048,4096]{0,1:T(8,128)(2,1)} %all-gather.3.cloned.1.call-done), kind=kOutput, calls=%fused_computation.2 | convolution fusion | flops 8600420352 | bytes 23068672 | tf_op jit(solution)/shard_map/dot_general | solution.py:17
  134.0 0.0 copy-start.2
  134.0 1.9 copy-done.2
  135.9 1.9 slice_bitcast_fusion.1
  137.8 1.4 copy.18
  139.2 7.1 fusion.30
  146.4 2.9 copy.19
  149.3 0.0 copy-start.6
  149.3 1.9 fusion.7
  151.2 2.2 multiply_convert_fusion.3
  153.4 40.8 %all-gather.5.cloned.1.call-done = bf16[1024,2048]{1,0:T(8,128)(2,1)} async-done(((bf16[16,2048]{1,0:T(8,128)(2,1)}), bf16[1024,2048]{1,0:T(8,128)(2,1)}) %all-gather.5.cloned.1.call-update) | async-done | bytes 4194320 | tf_op jit(solution)/shard_map/all_gather | solution.py:43
  194.2 0.0 copy-done
  194.2 0.0 copy-done.6
  194.2 7.3 select_convert_fusion.2
  201.5 2.3 convolution_convert_fusion
  203.8 0.0 copy-start.7
  203.8 1.3 copy-done.7
  205.2 5.7 fusion.9
  210.8 0.0 copy-start.3
  210.8 0.0 copy-start.8
  210.8 0.0 all-reduce.2.cloned.1.call-update
  210.8 0.0 reduce-scatter.2.cloned.1.call-start
  210.9 0.6 copy-done.3
  211.5 0.6 convert_reduce_fusion.1
  212.1 64.3 %psum.15 = f32[]{:T(128)} all-reduce(f32[]{:T(128)} %convert_reduce_fusion.1), channel_id=1, replica_groups=mesh['dp'=64,'pair'=2] {'dp','pair'}, use_global_device_ids=true, to_apply=%region_6.7 | all-reduce | flops 1 | bytes 8 | tf_op jit(solution)/shard_map/psum | solution.py:15
  276.4 93.3 %all-reduce.2.cloned.1.call-done = f32[1024,2048]{1,0:T(8,128)} async-done(((f32[1024,2048]{1,0:T(8,128)}), f32[1024,2048]{1,0:T(8,128)}) %all-reduce.2.cloned.1.call-update) | async-done | bytes 8388624 | tf_op jit(solution)/shard_map/psum | solution.py:62
  369.7 0.0 copy-done.8
  369.7 0.0 copy-start.5
  369.7 6.7 fusion.12
  376.4 0.0 copy-done.5
  376.4 0.0 copy-start.4
  376.4 3.3 multiply_reduce_fusion
  379.7 0.0 copy-done.4
  379.7 0.6 select_reduce_fusion
  380.3 5.7 fusion.5
  386.0 0.0 copy-start.1
  386.0 0.0 reduce-scatter.2.cloned.1.call-update
  386.9 648.0 %reduce-scatter.2.cloned.1.call-done = f32[8,2048]{1,0:T(8,128)} async-done(((f32[1024,2048]{1,0:T(8,128)}), f32[8,2048]{1,0:T(8,128)}) %reduce-scatter.2.cloned.1.call-update) | async-done | bytes 65552 | tf_op jit(solution)/shard_map/reduce_scatter | solution.py:73
  1034.9 1.5 broadcast_divide_fusion.2
  1036.4 0.0 copy-done.1
  (4 shorter events, 0.0 us)
Async XLA Ops:
  7.2 187.0 %copy-start = (bf16[512,2048]{1,0:T(8,128)(2,1)S(1)}, bf16[512,2048]{1,0:T(8,128)(2,1)}, u32[]{:S(2)}) copy-start(bf16[512,2048]{1,0:T(8,128)(2,1)} %param.11) | copy-start | bytes 6291460
  7.2 112.9 %all-gather.3.cloned.1.call-start = ((), (), s32[]{:S(2)}) async-start(), calls=%async_computation.1 | async-start | bytes 17039360 | tf_op jit(solution)/shard_map/all_gather | solution.py:18
  7.9 186.3 %all-gather.5.cloned.1.call-start = ((), (), s32[]{:S(2)}) async-start(), calls=%async_computation.2 | async-start | bytes 4259840 | tf_op jit(solution)/shard_map/all_gather | solution.py:43
  8.7 361.1 %all-reduce.2.cloned.1.call-start = ((), (), s32[]{:S(2)}) async-start(), calls=%async_computation.3 | async-start | bytes 16777216 | tf_op jit(solution)/shard_map/psum | solution.py:62
  134.0 1.9 copy-start.2
  149.3 44.9 %copy-start.6 = (s32[512]{0:T(512)S(1)}, s32[512]{0:T(512)}, u32[]{:S(2)}) copy-start(s32[512]{0:T(512)} %param.12) | copy-start | bytes 6148
  203.8 1.4 copy-start.7
  210.8 0.7 copy-start.3
  210.8 158.9 %copy-start.8 = (bf16[512,2048]{1,0:T(8,128)(2,1)S(1)}, bf16[512,2048]{1,0:T(8,128)(2,1)}, u32[]{:S(2)}) copy-start(bf16[512,2048]{1,0:T(8,128)(2,1)} %copy-done.7) | copy-start | bytes 6291460
  210.8 824.1 %reduce-scatter.2.cloned.1.call-start = ((), (), s32[]{:S(2)}) async-start(), calls=%async_computation.4 | async-start | bytes 8454144 | tf_op jit(solution)/shard_map/reduce_scatter | solution.py:73
  369.7 6.7 copy-start.5
  376.4 3.3 copy-start.4
  386.0 650.3 %copy-start.1 = (bf16[512,2048]{1,0:T(8,128)(2,1)S(1)}, bf16[512,2048]{1,0:T(8,128)(2,1)}, u32[]{:S(2)}) copy-start(bf16[512,2048]{1,0:T(8,128)(2,1)} %param.11) | copy-start | bytes 6291460
Sparse Core Ops, SparseCore 0:
  11.2 108.8 all-gather.2
  123.2 70.9 all-gather.4
  211.0 158.7 all-reduce.1
  386.2 648.6 reduce-scatter.1
where the time goes:
time: 1040 us
  waiting for transfers between devices  893 us (86%)
  blocking collectives  64.3 us (6%)
  matrix products  52 us (5%)
  between operations  14.7 us (1%)
    reduce_scatter x1, waiting for transfers between devices, on_device(): lax.psum_scatter(lax.dot_general(columns, scaled, (((0,), (0,)), ((), ())...  648 us
    all_gather x1, waiting for transfers between devices, on_device(): lax.all_gather(w_uvqk, 'dp', axis=1, tiled=True)  110 us
    psum x1, waiting for transfers between devices, on_device(): unif_sum = lax.psum(local_unif, ('dp', 'pair'))  93.3 us
    psum x1, blocking collectives, on_device(): n_unif = lax.psum(jnp.sum(flag), ('dp', 'pair'))  64.3 us
    all_gather x1, waiting for transfers between devices, on_device(): lax.all_gather(w_out, 'dp', axis=0, tiled=True)  40.8 us
  transfers between devices with their start and end apart: 4, of which 4 were waited for; matrix products, arithmetic and copies ran while one was open for 3% of the time, Pallas kernels for 0%

commit v1 on v0

v1 whole, which is shorter than its diff:
```python
import jax
import jax.numpy as jnp
from jax import lax
from jax.sharding import Mesh
from jax.sharding import PartitionSpec as P

HEADS = 8
DH = 128
AXES = ("y", "zh", "x", "c", "zl")
CHIPS = ("y", "zh", "x", "zl")
SWAP = [(0, 1), (1, 0)]


def split_core(parts):
    core = lax.axis_index("c")
    away = lax.dynamic_index_in_dim(parts, 1 - core, 0, keepdims=False)
    mine = lax.dynamic_index_in_dim(parts, core, 0, keepdims=False)
    came = lax.ppermute(away, "c", SWAP)
    return (mine.astype(jnp.float32) + came.astype(jnp.float32)).astype(jnp.bfloat16)


def scatter_chips(half):
    rows = half.shape[0] // 64
    got = lax.all_to_all(half.reshape(64, rows, -1), CHIPS, 0, 0, tiled=True)
    return jnp.sum(got.astype(jnp.float32), axis=0)


def gather_chips(rows):
    got = lax.all_to_all(jnp.broadcast_to(rows[None], (64,) + rows.shape), CHIPS, 0, 0, tiled=True)
    return got.reshape(64 * rows.shape[0], -1)


def on_device(events, w_uvqk, w_out, targets, item_ids, uniform_flags, lengths, seq_weights):
    count = events.shape[0]
    width = HEADS * DH
    seq_max = count // 4
    core = lax.axis_index("c")
    flag = uniform_flags.astype(jnp.float32)
    counts = lax.all_to_all(jnp.broadcast_to(jnp.sum(flag), (128, 128)), AXES, 0, 0, tiled=True)
    n_unif = jnp.sum(counts[:, 0])
    n_train = jnp.float32(count * 128) - n_unif
    dp = ("y", "zh", "x", "c")
    pre = jnp.dot(
        events, lax.all_gather(w_uvqk, dp, axis=1, tiled=True), preferred_element_type=jnp.float32
    )
    uvqk = jax.nn.silu(pre).astype(jnp.bfloat16)
    gate_u = uvqk[:, 0:width]
    vals = uvqk[:, width : 2 * width].reshape(count, HEADS, DH)
    query = uvqk[:, 2 * width : 3 * width].reshape(count, HEADS, DH)
    keys = uvqk[:, 3 * width : 4 * width].reshape(count, HEADS, DH)
    place = jnp.arange(count, dtype=jnp.int32)
    ends = jnp.cumsum(lengths[0])
    seqid = jnp.sum((place[:, None] >= ends[None, :]).astype(jnp.int32), axis=1)
    allowed = (seqid[:, None] == seqid[None, :]) & (place[:, None] >= place[None, :])
    scores_att = jnp.einsum(
        "ihd,jhd->hij", query, keys, preferred_element_type=jnp.float32
    ) / jnp.sqrt(jnp.float32(DH))
    probs = jnp.where(allowed[None], jax.nn.silu(scores_att) / seq_max, 0.0).astype(jnp.bfloat16)
    attn = jnp.einsum("hij,jhd->ihd", probs, vals, preferred_element_type=jnp.float32).reshape(
        count, width
    )
    mean = jnp.mean(attn, axis=1, keepdims=True)
    var = jnp.mean((attn - mean) ** 2, axis=1, keepdims=True)
    mixed = ((attn - mean) * lax.rsqrt(var + 1e-05) * gate_u.astype(jnp.float32)).astype(
        jnp.bfloat16
    )
    summed = jnp.dot(
        mixed, lax.all_gather(w_out, dp, axis=0, tiled=True), preferred_element_type=jnp.float32
    )
    outputs = (events.astype(jnp.float32) + summed).astype(jnp.bfloat16)
    scores = jnp.dot(outputs, targets.T, preferred_element_type=jnp.float32)
    diag = place[:, None] == place[None, :]
    other = item_ids[:, None] != item_ids[None, :]
    coef = jnp.where(
        diag, -jax.nn.sigmoid(-scores), jnp.where(other, jax.nn.sigmoid(scores) / count, 0.0)
    ).astype(jnp.bfloat16)
    grad_out = jnp.dot(coef, targets, preferred_element_type=jnp.float32).astype(jnp.bfloat16)
    member = (seqid[:, None] == jnp.arange(seq_weights.shape[0], dtype=jnp.int32)[None, :]).astype(
        jnp.float32
    )
    weight_row = jnp.sum(member * seq_weights[None, :], axis=1) * (1.0 - flag)
    scaled = (grad_out.astype(jnp.float32) * weight_row[:, None]).astype(jnp.bfloat16)
    unif_rows = grad_out * uniform_flags[:, None].astype(jnp.bfloat16)
    contract = (((0,), (0,)), ((), ()))
    local_unif = lax.dot_general(mixed, unif_rows, contract, preferred_element_type=jnp.float32)
    half_unif = split_core(local_unif.astype(jnp.bfloat16).reshape(2, 512, -1))
    unif_rows_sum = scatter_chips(half_unif).astype(jnp.bfloat16)
    unif_mine = gather_chips(unif_rows_sum)
    unif_away = lax.ppermute(unif_mine, "c", SWAP)
    mixed_mine = lax.dynamic_slice_in_dim(mixed, core * 512, 512, 1)
    mixed_away = lax.dynamic_slice_in_dim(mixed, (1 - core) * 512, 512, 1)
    proj_mine = jnp.dot(grad_out, unif_mine.T, preferred_element_type=jnp.float32)
    proj_away = jnp.dot(grad_out, unif_away.T, preferred_element_type=jnp.float32)
    per_row = jnp.sum(mixed_mine.astype(jnp.float32) * proj_mine, axis=1) + jnp.sum(
        mixed_away.astype(jnp.float32) * proj_away, axis=1
    )
    per_row = -per_row * (1.0 - flag) / n_unif
    hyper = jnp.sum(member * per_row[:, None], axis=0)
    local_w = lax.dot_general(mixed, scaled, contract, preferred_element_type=jnp.float32)
    parts_w = local_w.astype(jnp.bfloat16).reshape(32, 2, 16, -1).transpose(1, 0, 2, 3)
    half_w = split_core(parts_w.reshape(2, 512, -1))
    weighted_grad = scatter_chips(half_w) / n_train
    return (hyper, weighted_grad)


def solution(mesh):
    fine = Mesh(mesh.devices.reshape(4, 2, 4, 2, 2), AXES)
    dp = ("y", "zh", "x", "c")
    return jax.shard_map(
        on_device,
        mesh=fine,
        in_specs=(
            P(AXES, None),
            P(None, dp),
            P(dp, None),
            P(AXES, None),
            P(AXES),
            P(AXES),
            P(AXES, None),
            P(AXES),
        ),
        out_specs=(P(AXES), P(AXES, None)),
        check_vma=False,
    )
```

time: 1040 us -> 369 us (0.35)
  waiting for transfers between devices: 893 us -> 201 us
  starting transfers between devices: 0.16 us -> 10.8 us
    reduce_scatter x1 -> x0, waiting for transfers between devices: 648 us -> none  [on_device(): lax.psum_scatter(lax.dot_general(columns, scaled, (((0,), (0,)), ((), ())...]
    psum x1 -> x0, waiting for transfers between devices: 93.3 us -> none  [on_device(): unif_sum = lax.psum(local_unif, ('dp', 'pair'))]
    all_to_all x0 -> x2, blocking collectives: none -> 70.4 us  [the longest x1 36.2 us: scatter_chips(): got = lax.all_to_all(half.reshape(64, rows, -1), CHIPS, 0, 0, tiled=True)]
    psum x1 -> x0, blocking collectives: 64.3 us -> none  [on_device(): n_unif = lax.psum(jnp.sum(flag), ('dp', 'pair'))]
    all_to_all x0 -> x2, waiting for transfers between devices: none -> 39 us  [the longest x1 29.9 us: scatter_chips(): got = lax.all_to_all(half.reshape(64, rows, -1), CHIPS, 0, 0, tiled=True)]
  transfers between devices with their start and end apart: 4 -> 7, of which waited for: 4 -> 6; matrix products, arithmetic and copies ran while one was open for 3% -> 11% of each run, Pallas kernels for 0% -> 0%
where the time goes in v1:
time: 369 us
  waiting for transfers between devices  201 us (54%)
  blocking collectives  70.4 us (19%)
  matrix products  42.3 us (11%)
  other arithmetic  17.5 us (5%)
  between operations  14.9 us (4%)
  local copies, waits for them, and re-layouts  12 us (3%)
  starting transfers between devices  10.8 us (3%)
    all_gather x1, waiting for transfers between devices, on_device(): lax.all_gather(w_uvqk, dp, axis=1, tiled=True)  110 us
    all_gather x1, waiting for transfers between devices, on_device(): lax.all_gather(w_out, dp, axis=0, tiled=True)  42.3 us
    all_to_all x1, blocking collectives, scatter_chips(): got = lax.all_to_all(half.reshape(64, rows, -1), CHIPS, 0, 0, tiled=True)  36.2 us
    all_to_all x1, blocking collectives, gather_chips(): lax.all_to_all(jnp.broadcast_to(rows[None], (64,) + rows.shape), CHIPS, 0...  34.1 us
    all_to_all x1, waiting for transfers between devices, scatter_chips(): got = lax.all_to_all(half.reshape(64, rows, -1), CHIPS, 0, 0, tiled=True)  29.9 us
    dot_general x1, matrix products, on_device(): jnp.dot(events, lax.all_gather(w_uvqk, dp, axis=1, tiled=True), preferred...  13.9 us
    all_to_all x1, waiting for transfers between devices, on_device(): lax.all_to_all(jnp.broadcast_to(jnp.sum(flag), (128, 128)), AXES, 0, 0, t...  9.09 us
    ppermute x2, waiting for transfers between devices, split_core(): came = lax.ppermute(away, 'c', SWAP)  8.39 us
  transfers between devices with their start and end apart: 7, of which 6 were waited for; matrix products, arithmetic and copies ran while one was open for 11% of the time, Pallas kernels for 0%

profile of v1, /device:TPU:0, one launch (start us, length us, event | category | flops | bytes accessed | tf_op | source)
XLA Modules:
  0.0 368.6 jit_solution(8549933282857203315)
XLA Ops:
  7.2 0.0 copy-start
  7.2 0.0 all-gather.3.cloned.1.call-start
  7.2 0.7 all-gather.3.cloned.1.call-update
  7.9 0.0 all-gather.5.cloned.1.call-start
  8.0 0.7 all-gather.5.cloned.1.call-update
  8.7 0.7 convert_element_type.92
  9.4 0.8 reduce-window.8
  10.2 0.1 convert_reduce_fusion.1
  10.3 0.2 fusion.22
  10.5 109.6 %all-gather.3.cloned.1.call-done = bf16[2048,4096]{0,1:T(8,128)(2,1)} async-done(((bf16[2048,64]{0,1:T(8,128)(2,1)}), bf16[2048,4096]{0,1:T(8,128)(2,1)}) %all-gather.3.cloned.1.call-update) | async-done | bytes 16777232 | tf_op jit(solution)/shard_map/all_gather | solution.py:44
  120.1 13.9 %multiply_convert_fusion = bf16[512,4096]{1,0:T(8,128)(2,1)S(1)} fusion(bf16[512,2048]{1,0:T(8,128)(2,1)} %param.8, bf16[2048,4096]{0,1:T(8,128)(2,1)} %all-gather.3.cloned.1.call-done), kind=kOutput, calls=%fused_computation.1 | convolution fusion | flops 8600420352 | bytes 23068672 | tf_op jit(solution)/shard_map/dot_general | solution.py:43
  134.0 0.0 copy-start.2
  134.0 2.3 slice_bitcast_fusion.1
  136.3 0.2 copy-done.2
  136.6 1.4 copy.40
  137.9 7.1 %fusion.30 = (f32[512]{0:T(512)S(1)}, f32[8,128,512]{2,1,0:T(8,128)}) fusion(bf16[512,8,128]{0,2,1:T(8,128)(2,1)} %bitcast.69, pred[512,512]{1,0:T(8,128)(4,1)S(1)} %fusion.22, bf16[64,8,8,128]{3,2,1,0:T(8,128)(2,1)} %get-tuple-element.5, bf16[64,8,8,128]{3,2,1,0:T(8,128)(2,1)} %get-tuple-element.4), kind=kOutput, calls=%fused_computation.58 | convolution fusion | flops 1091042816 | bytes 5507072 | tf_op jit(solution)/shard_map/hij,jhd->ihd/dot_general | solution.py:59
  145.1 2.9 copy.41
  148.0 0.0 copy-start.1
  148.0 2.0 fusion.8
  150.0 0.2 copy-done.1
  150.2 1.6 multiply_convert_fusion.3
  151.9 42.3 %all-gather.5.cloned.1.call-done = bf16[1024,2048]{1,0:T(8,128)(2,1)} async-done(((bf16[16,2048]{1,0:T(8,128)(2,1)}), bf16[1024,2048]{1,0:T(8,128)(2,1)}) %all-gather.5.cloned.1.call-update) | async-done | bytes 4194320 | tf_op jit(solution)/shard_map/all_gather | solution.py:68
  194.2 0.0 copy-done
  194.2 0.0 copy-done.6
  194.2 7.3 %select_convert_fusion.2 = bf16[512,512]{1,0:T(8,128)(2,1)} fusion(bf16[512,2048]{1,0:T(8,128)(2,1)S(1)} %copy-done, bf16[512,2048]{1,0:T(8,128)(2,1)} %param.8, bf16[512,1024]{1,0:T(8,128)(2,1)S(1)} %multiply_convert_fusion.3, bf16[1024,2048]{1,0:T(8,128)(2,1)} %all-gather.5.cloned.1.call-done, s32[512]{0:T(512)S(1)} %copy-done.6), kind=kOutput, calls=%fused_computation.35 | convolution fusion | flops 3227516928 | bytes 9963520 | tf_op jit(solution)/shard_map/dot_general | solution.py:71
  201.5 2.3 convolution_convert_fusion.2
  203.8 0.0 copy-start.7
  203.8 2.4 convolution_convert_fusion.1
  206.3 0.0 copy-done.7
  206.3 0.0 copy-start.3
  206.3 1.8 dynamic-slice_bitcast_fusion.1
  208.1 0.9 copy-done.3
  209.0 0.3 collective-permute-start
  209.2 4.2 %collective-permute-done = bf16[512,2048]{1,0:T(8,128)(2,1)} collective-permute-done((bf16[512,2048]{1,0:T(8,128)(2,1)}, bf16[512,2048]{1,0:T(8,128)(2,1)}, u32[]{:S(2)}, u32[]{:S(2)}) %collective-permute-start) | collective-permute-done | bytes 2097184 | tf_op jit(solution)/shard_map/ppermute | solution.py:18
  213.5 3.0 fusion.5
  216.5 36.2 %all_to_all.24 = bf16[64,8,2048]{2,1,0:T(8,128)(2,1)} all-to-all(bf16[64,8,2048]{2,1,0:T(8,128)(2,1)S(1)} %fusion.5), channel_id=1, replica_groups=mesh['y'=4,'zh'=2,'x'=4,'c'=2,'zl'=2] {'y','zh','x','zl'}, dimensions={0} | all-to-all | bytes 4194304 | tf_op jit(solution)/shard_map/all_to_all | solution.py:24
  252.7 1.9 reduce_sum.105
  254.6 0.2 broadcast_in_dim.22
  254.9 0.0 copy-start.4
  254.9 34.1 %all_to_all.25 = bf16[64,8,2048]{2,1,0:T(8,128)(2,1)} all-to-all(bf16[64,8,2048]{2,1,0:T(8,128)(2,1)S(1)} %broadcast_in_dim.22), channel_id=1, replica_groups=mesh['y'=4,'zh'=2,'x'=4,'c'=2,'zl'=2] {'y','zh','x','zl'}, dimensions={0} | all-to-all | bytes 4194304 | tf_op jit(solution)/shard_map/all_to_all | solution.py:29
  289.0 0.0 collective-permute-start.1
  289.0 0.0 copy-done.4
  289.0 0.6 convert_reduce_fusion.2
  289.6 1.3 broadcast_in_dim.24
  290.9 4.8 %all-to-all-start.2 = ((f32[128,1,128]{2,1,0:T(1,128)}), f32[128,1,128]{2,1,0:T(1,128)S(1)}, u32[]{:S(2)}, u32[]{:S(2)}) async-start(f32[128,1,128]{2,1,0:T(1,128)} %broadcast_in_dim.24), calls=%async_computation.2 | async-start | bytes 131072 | tf_op jit(solution)/shard_map/all_to_all | solution.py:39
  295.8 9.1 %all-to-all-done.2 = f32[128,1,128]{2,1,0:T(1,128)S(1)} async-done(((f32[128,1,128]{2,1,0:T(1,128)}), f32[128,1,128]{2,1,0:T(1,128)S(1)}, u32[]{:S(2)}, u32[]{:S(2)}) %all-to-all-start.2) | async-done | bytes 65568 | tf_op jit(solution)/shard_map/all_to_all | solution.py:39
  304.8 0.6 slice_reduce_fusion
  305.5 3.7 %fusion.11 = f32[512]{0:T(512)S(1)} fusion(bf16[512,2048]{1,0:T(8,128)(2,1)} %copy-done.7, bf16[512,1024]{1,0:T(8,128)(2,1)S(1)} %multiply_convert_fusion.3, s32[]{:T(128)S(6)} %select_n.28, bf16[64,8,2048]{2,1,0:T(8,128)(2,1)} %all_to_all.25), kind=kOutput, calls=%fused_computation.26 | convolution fusion | flops 1074527744 | bytes 4720644 | tf_op jit(solution)/shard_map/dot_general | solution.py:92
  309.2 0.0 collective-permute-done.1
  309.2 0.0 copy-done.8
  309.2 3.0 fusion.12
  312.2 0.7 multiply_divide_fusion
  312.9 0.0 copy-done.5
  312.9 0.6 select_reduce_fusion
  313.5 2.5 convolution_convert_fusion
  316.0 0.6 copy.37
  316.6 0.1 dynamic-slice_bitcast_fusion
  316.7 0.1 collective-permute-start.2
  316.8 4.1 %collective-permute-done.2 = bf16[512,2048]{1,0:T(8,128)(2,1)S(1)} collective-permute-done((bf16[512,2048]{1,0:T(8,128)(2,1)S(1)}, bf16[512,2048]{1,0:T(8,128)(2,1)S(1)}, u32[]{:S(2)}, u32[]{:S(2)}) %collective-permute-start.2) | collective-permute-done | bytes 2097184 | tf_op jit(solution)/shard_map/ppermute | solution.py:18
  321.0 2.1 fusion.6
  323.1 5.6 %all-to-all-start.3 = ((bf16[64,8,2048]{2,1,0:T(8,128)(2,1)}), bf16[64,8,2048]{2,1,0:T(8,128)(2,1)}, u32[]{:S(2)}, u32[]{:S(2)}) async-start(bf16[64,8,2048]{2,1,0:T(8,128)(2,1)} %fusion.6), calls=%async_computation.3 | async-start | bytes 4194304 | tf_op jit(solution)/shard_map/all_to_all | solution.py:24
  329.3 29.9 %all-to-all-done.3 = bf16[64,8,2048]{2,1,0:T(8,128)(2,1)} async-done(((bf16[64,8,2048]{2,1,0:T(8,128)(2,1)}), bf16[64,8,2048]{2,1,0:T(8,128)(2,1)}, u32[]{:S(2)}, u32[]{:S(2)}) %all-to-all-start.3) | async-done | bytes 2097184 | tf_op jit(solution)/shard_map/all_to_all | solution.py:24
  359.2 1.9 convert_reduce_fusion
  361.1 0.6 broadcast_divide_fusion
  (6 shorter events, 0.0 us)
Async XLA Ops:
  7.2 187.0 %copy-start = (bf16[512,2048]{1,0:T(8,128)(2,1)S(1)}, bf16[512,2048]{1,0:T(8,128)(2,1)}, u32[]{:S(2)}) copy-start(bf16[512,2048]{1,0:T(8,128)(2,1)} %param.11) | copy-start | bytes 6291460
  7.2 112.9 %all-gather.3.cloned.1.call-start = ((), (), s32[]{:S(2)}) async-start(), calls=%async_computation.4 | async-start | bytes 17039360 | tf_op jit(solution)/shard_map/all_gather | solution.py:44
  7.9 186.3 %all-gather.5.cloned.1.call-start = ((), (), s32[]{:S(2)}) async-start(), calls=%async_computation.5 | async-start | bytes 4259840 | tf_op jit(solution)/shard_map/all_gather | solution.py:68
  134.0 2.5 copy-start.2
  148.0 2.2 copy-start.1
  150.2 44.0 %copy-start.6 = (s32[512]{0:T(512)S(1)}, s32[512]{0:T(512)}, u32[]{:S(2)}) copy-start(s32[512]{0:T(512)} %param.12) | copy-start | bytes 6148
  203.8 2.5 copy-start.7
  206.3 2.7 copy-start.3
  209.0 4.5 %collective-permute-start = (bf16[512,2048]{1,0:T(8,128)(2,1)}, bf16[512,2048]{1,0:T(8,128)(2,1)}, u32[]{:S(2)}, u32[]{:S(2)}) collective-permute-start(bf16[512,2048]{1,0:T(8,128)(2,1)} %dynamic-slice_bitcast_fusion.1), channel_id=1, source_target_pairs={{0,2},{2,0},{1,3},{3,1},{4,6},{6,4},{5,7},{7,5},{8,10},{10,8},{9,1... | collective-permute-start | bytes 6291464 | tf_op jit(solution)/shard_map/ppermute | solution.py:18
  254.9 34.1 %copy-start.4 = (s32[512]{0:T(512)S(1)}, s32[512]{0:T(512)}, u32[]{:S(2)}) copy-start(s32[512]{0:T(512)} %param.13) | copy-start | bytes 6148
  289.0 20.2 %collective-permute-start.1 = (bf16[512,2048]{1,0:T(8,128)(2,1)}, bf16[512,2048]{1,0:T(8,128)(2,1)}, u32[]{:S(2)}, u32[]{:S(2)}) collective-permute-start(bf16[512,2048]{1,0:T(8,128)(2,1)} %bitcast.9), channel_id=1, source_target_pairs={{0,2},{2,0},{1,3},{3,1},{4,6},{6,4},{5,7},{7,5},{8,10},{10,8},{9,1... | collective-permute-start | bytes 6291464 | tf_op jit(solution)/shard_map/ppermute | solution.py:89
  290.9 13.9 %all-to-all-start.2 = ((f32[128,1,128]{2,1,0:T(1,128)}), f32[128,1,128]{2,1,0:T(1,128)S(1)}, u32[]{:S(2)}, u32[]{:S(2)}) async-start(f32[128,1,128]{2,1,0:T(1,128)} %broadcast_in_dim.24), calls=%async_computation.2 | async-start | bytes 131072 | tf_op jit(solution)/shard_map/all_to_all | solution.py:39
  305.5 3.8 %copy-start.8 = (bf16[512,2048]{1,0:T(8,128)(2,1)S(1)}, bf16[512,2048]{1,0:T(8,128)(2,1)}, u32[]{:S(2)}) copy-start(bf16[512,2048]{1,0:T(8,128)(2,1)} %copy-done.7) | copy-start | bytes 6291460
  309.2 3.7 copy-start.5
  316.7 4.2 %collective-permute-start.2 = (bf16[512,2048]{1,0:T(8,128)(2,1)S(1)}, bf16[512,2048]{1,0:T(8,128)(2,1)S(1)}, u32[]{:S(2)}, u32[]{:S(2)}) collective-permute-start(bf16[512,2048]{1,0:T(8,128)(2,1)S(1)} %dynamic-slice_bitcast_fusion), channel_id=1, source_target_pairs={{0,2},{2,0},{1,3},{3,1},{4,6},{6,4},{5,7},{7,5},{8,10},{10,8},{9,1... | collective-permute-start | bytes 6291464 | tf_op jit(solution)/shard_map/ppermute | solution.py:18
  323.1 36.1 %all-to-all-start.3 = ((bf16[64,8,2048]{2,1,0:T(8,128)(2,1)}), bf16[64,8,2048]{2,1,0:T(8,128)(2,1)}, u32[]{:S(2)}, u32[]{:S(2)}) async-start(bf16[64,8,2048]{2,1,0:T(8,128)(2,1)} %fusion.6), calls=%async_computation.3 | async-start | bytes 4194304 | tf_op jit(solution)/shard_map/all_to_all | solution.py:24
Sparse Core Ops, SparseCore 0:
  11.2 108.8 all-gather.2
  123.2 70.9 all-gather.4
